TPU v7x, 32 devices: a whole 2x2x4 slice. The times are simulated.
32 devices in a mesh: frames: 2 (over x), date: 16 (over z, y, core).
Axes of the slice: x: 2, y: 2, z: 4, core: 2. Of those that a mesh axis runs over, the one named last changes fastest.
Arguments:
- slc: float32 [2, 256, 288, 48], P(None, 'date', 'frames'), parts along dimension 2, may hold values from -6 to 6
Outputs:
- coherence: bfloat16 [96, 8, 256, 256], P(('frames', 'date')), parts along dimension 0
There are 2 independent parts, one for each index of `frames`. A program takes and returns all parts, laid end to end along the dimension named above; each array names one. Nothing has to cross between parts.
All inputs are finite; a program needn't handle non-finite values.
Results may differ from a plain program's by a relative error of at most 0.001.
Values sent between devices are 32-bit elements; how exact they have to be, the bound alone decides.
A program may use at most 128 MiB of HBM per device.

v0:
```python
import jax
import jax.numpy as jnp
from jax import lax
from jax.sharding import PartitionSpec as P

BOX_AZ = 11
BOX_RG = 23
STEP_AZ = 3
STEP_RG = 6
MARGIN = 8


def from_behind(value, axis, steps):
    count = lax.axis_size(axis)
    first, last = (max(0, -steps), min(count, count - steps))
    return lax.ppermute(value, axis, [(source, source + steps) for source in range(first, last)])


def coherence_rows(with_margin, out_rows):
    date_count = with_margin.shape[1]
    range_width = with_margin.shape[3]
    range_cols = range_width // STEP_RG
    stacked = with_margin.reshape(2 * date_count, with_margin.shape[2] * range_width)
    span = BOX_AZ * range_width
    column = lax.broadcasted_iota(jnp.int32, (range_cols, span), 1) % range_width
    first = lax.broadcasted_iota(jnp.int32, (range_cols, span), 0) * STEP_RG
    inside = ((column >= first) & (column < first + BOX_RG)).astype(stacked.dtype)
    lower = lax.broadcasted_iota(jnp.int32, (date_count, date_count), 0)
    upper = lax.broadcasted_iota(jnp.int32, (date_count, date_count), 1)

    def one_row(row_index):
        start = row_index * (STEP_AZ * range_width)
        window = lax.dynamic_slice_in_dim(stacked, start, span, 1)
        masked = inside[:, None, :] * window[None]
        gram = jnp.einsum("rak,bk->rab", masked, window, precision=lax.Precision.HIGHEST)
        real_part = gram[:, :date_count, :date_count] + gram[:, date_count:, date_count:]
        imag_part = gram[:, date_count:, :date_count] - gram[:, :date_count, date_count:]
        powers = jnp.diagonal(real_part, axis1=1, axis2=2)
        inverse = 1.0 / jnp.sqrt(powers)
        scale = inverse[:, :, None] * inverse[:, None, :]
        packed = jnp.where((upper >= lower)[None], real_part * scale, imag_part * scale)
        return packed.astype(jnp.bfloat16)

    return lax.map(one_row, jnp.arange(out_rows, dtype=jnp.int32))


def on_device(slc):
    slab_count = lax.axis_size("date")
    slab_height = slc.shape[2] // slab_count
    slab_pixels = lax.all_to_all(slc, "date", split_axis=2, concat_axis=1, tiled=True)
    below_rows = from_behind(slab_pixels[:, :, :MARGIN, :], "date", -1)
    with_margin = jnp.concatenate([slab_pixels, below_rows], axis=2)
    return coherence_rows(with_margin, slab_height // STEP_AZ)


def solution(mesh):
    in_specs = (P(None, "date", "frames", None),)
    out_specs = P(("frames", "date"), None, None, None)
    return jax.shard_map(
        on_device, mesh=mesh, in_specs=in_specs, out_specs=out_specs, check_vma=False
    )
```

profile of v0, /device:TPU:9, one launch (start us, length us, event | category | flops | bytes accessed | tf_op | source)
XLA Modules:
  0.0 226.5 jit_solution(1379762337118544538)
XLA Ops:
  0.0 2.6 %copy.29 = f32[2,16,144,48]{3,1,0,2:T(8,128)S(1)} copy(f32[2,16,144,48]{2,3,1,0:T(8,128)} %param.3) | data formatting | bytes 1769472 | tf_op args[0]
  4.9 28.4 %all_to_all.18 = f32[16,1,13824]{2,1,0:T(1,128)S(1)} all-to-all(f32[16,1,13824]{2,1,0:T(1,128)S(1)} %reshape.41), channel_id=1, replica_groups=mesh['frames'=2,'date'=16] {'date'}, dimensions={0} | all-to-all | bytes 1769472 | tf_op jit(solution)/shard_map/all_to_all | solution.py:50
  33.8 2.7 %reduce = f32[16,13824]{1,0:T(8,128)S(1)} reduce(f32[16,1,13824]{2,1,0:T(1,128)S(1)} %all_to_all.18, f32[]{:T(128)} %broadcast.46), dimensions={1}, to_apply=%all_to_all.13.reduce_sub_computation | reduce | bytes 1769476 | tf_op jit(solution)/shard_map/all_to_all | solution.py:50
  36.5 2.4 %reshape.42 = f32[144,2,16,48]{3,2,1,0:T(8,128)} reshape(f32[16,13824]{1,0:T(8,128)S(1)} %reduce) | data formatting | bytes 1769472
  46.5 11.4 %collective-permute-done = f32[2,256,8,48]{1,3,2,0:T(8,128)} collective-permute-done((f32[2,256,8,48]{1,3,2,0:T(8,128)S(1)}, f32[2,256,8,48]{1,3,2,0:T(8,128)}, u32[]{:S(2)}, u32[]{:S(2)}) %collective-permute-start) | collective-permute-done | bytes 786464 | tf_op jit(solution)/shard_map/ppermute | solution.py:16
  57.9 3.1 %copy.33 = f32[2,256,8,48]{3,1,2,0:T(8,128)} copy(f32[2,256,8,48]{1,3,2,0:T(8,128)} %collective-permute-done) | data formatting | bytes 1572864 | tf_op jit(solution)/shard_map/ppermute | solution.py:16
  61.0 4.1 %pad_maximum_fusion = f32[2,256,17,48]{3,1,2,0:T(8,128)} fusion(f32[2,256,8,48]{3,1,2,0:T(8,128)} %copy.33, f32[2,256,9,48]{3,1,2,0:T(8,128)S(1)} %bitcast.39), kind=kLoop, calls=%fused_computation.25 | loop fusion | flops 417792 | bytes 3342336 | tf_op jit(solution)/shard_map/concatenate | solution.py:52
  65.1 4.7 %copy.34 = f32[2,256,17,48]{1,0,3,2:T(2,128)S(1)} copy(f32[2,256,17,48]{3,1,2,0:T(8,128)} %pad_maximum_fusion) | data formatting | bytes 3342336 | tf_op jit(solution)/shard_map/concatenate | solution.py:52
  69.9 156.6 %while.13 = (s32[]{:T(128)}, bf16[3,8,256,256]{3,2,1,0:T(8,128)(2,1)}, s32[3]{0:T(128)S(1)}, f32[512,816]{0,1:T(8,128)S(1)}, s32[8]{0:T(128)S(1)}, /*index=5*/s3...) while((s32[]{:T(128)}, ...), condition=%wide.region_1.2_spmd.clone, body=%wide.region_0.1_spmd.clone.sunk | while | flops 13294000128 | bytes 78718440 | solution.py:44
  71.6 23.2 %fusion.29 = f32[8,512,512]{2,1,0:T(8,128)S(1)} fusion(f32[512,528]{0,1:T(8,128)S(1)} %constant_dynamic-slice_fusion.2, f32[8,528]{1,0:T(8,128)S(1)} %fusion.28), kind=kOutput, calls=%fused_computation.3.clone.1 | convolution fusion | flops 13289717760 | bytes 9486848 | tf_op jit(solution)/shard_map/while/body/eval_jaxpr/rak,bk->rab/dot_general | solution.py:35
  94.9 3.2 %copy-done = f32[8,512,512]{2,1,0:T(8,128)} copy-done((f32[8,512,512]{2,1,0:T(8,128)}, f32[8,512,512]{2,1,0:T(8,128)S(1)}, u32[]{:S(2)}) %copy-start) | copy-done | bytes 8388632 | tf_op jit(solution)/shard_map/while
  98.3 16.7 %copy.39 = f32[8,256,256]{0,2,1:T(8,128)} copy(f32[8,256,256]{2,1,0:T(8,128)S(1)} %slice_add_fusion.2) | data formatting | bytes 4194304 | tf_op jit(solution)/shard_map/while/body/eval_jaxpr/add | solution.py:36
  115.0 2.3 %gather_fusion = f32[256,8]{1,0:T(8,128)S(1)} fusion(f32[8,256,256]{0,2,1:T(8,128)} %copy.39, s32[256]{0:T(256)S(1)} %bitcast.36), kind=kCustom, calls=%fused_computation.clone.clone.1 | custom fusion | bytes 18432 | tf_op jit(solution)/shard_map/while/body/eval_jaxpr/jit(diagonal)/gather | solution.py:38
  117.5 4.8 %fusion.31 = bf16[3,8,256,256]{3,2,1,0:T(8,128)(2,1)} fusion(bf16[3,8,256,256]{3,2,1,0:T(8,128)(2,1)} %get-tuple-element.203, s32[]{:T(128)} %get-tuple-element.202, f32[8,512,512]{2,1,0:T(8,128)} %copy-done, f32[8,256]{1,0:T(8,128)S(1)} %copy.40, pred[256,256]{1,0:T(8,128)(4,1)S(1)} %fusion.30), kind=kLoop, calls=%fused_computation.15.clone.1 | loop fusion | flops 3670016 | bytes 9519616 | tf_op jit(solution)/shard_map/while/body/jit(dynamic_update_index_in_dim)/dynamic_update_slice | solution.py:44
  123.8 23.2 %fusion.29 = f32[8,512,512]{2,1,0:T(8,128)S(1)} fusion(f32[512,528]{0,1:T(8,128)S(1)} %constant_dynamic-slice_fusion.2, f32[8,528]{1,0:T(8,128)S(1)} %fusion.28), kind=kOutput, calls=%fused_computation.3.clone.1 | convolution fusion | flops 13289717760 | bytes 9486848 | tf_op jit(solution)/shard_map/while/body/eval_jaxpr/rak,bk->rab/dot_general | solution.py:35
  147.0 3.2 %copy-done = f32[8,512,512]{2,1,0:T(8,128)} copy-done((f32[8,512,512]{2,1,0:T(8,128)}, f32[8,512,512]{2,1,0:T(8,128)S(1)}, u32[]{:S(2)}) %copy-start) | copy-done | bytes 8388632 | tf_op jit(solution)/shard_map/while
  150.5 16.7 %copy.39 = f32[8,256,256]{0,2,1:T(8,128)} copy(f32[8,256,256]{2,1,0:T(8,128)S(1)} %slice_add_fusion.2) | data formatting | bytes 4194304 | tf_op jit(solution)/shard_map/while/body/eval_jaxpr/add | solution.py:36
  167.1 2.3 %gather_fusion = f32[256,8]{1,0:T(8,128)S(1)} fusion(f32[8,256,256]{0,2,1:T(8,128)} %copy.39, s32[256]{0:T(256)S(1)} %bitcast.36), kind=kCustom, calls=%fused_computation.clone.clone.1 | custom fusion | bytes 18432 | tf_op jit(solution)/shard_map/while/body/eval_jaxpr/jit(diagonal)/gather | solution.py:38
  169.6 4.8 %fusion.31 = bf16[3,8,256,256]{3,2,1,0:T(8,128)(2,1)} fusion(bf16[3,8,256,256]{3,2,1,0:T(8,128)(2,1)} %get-tuple-element.203, s32[]{:T(128)} %get-tuple-element.202, f32[8,512,512]{2,1,0:T(8,128)} %copy-done, f32[8,256]{1,0:T(8,128)S(1)} %copy.40, pred[256,256]{1,0:T(8,128)(4,1)S(1)} %fusion.30), kind=kLoop, calls=%fused_computation.15.clone.1 | loop fusion | flops 3670016 | bytes 9519616 | tf_op jit(solution)/shard_map/while/body/jit(dynamic_update_index_in_dim)/dynamic_update_slice | solution.py:44
  175.9 23.2 %fusion.29 = f32[8,512,512]{2,1,0:T(8,128)S(1)} fusion(f32[512,528]{0,1:T(8,128)S(1)} %constant_dynamic-slice_fusion.2, f32[8,528]{1,0:T(8,128)S(1)} %fusion.28), kind=kOutput, calls=%fused_computation.3.clone.1 | convolution fusion | flops 13289717760 | bytes 9486848 | tf_op jit(solution)/shard_map/while/body/eval_jaxpr/rak,bk->rab/dot_general | solution.py:35
  199.1 3.2 %copy-done = f32[8,512,512]{2,1,0:T(8,128)} copy-done((f32[8,512,512]{2,1,0:T(8,128)}, f32[8,512,512]{2,1,0:T(8,128)S(1)}, u32[]{:S(2)}) %copy-start) | copy-done | bytes 8388632 | tf_op jit(solution)/shard_map/while
  202.6 16.7 %copy.39 = f32[8,256,256]{0,2,1:T(8,128)} copy(f32[8,256,256]{2,1,0:T(8,128)S(1)} %slice_add_fusion.2) | data formatting | bytes 4194304 | tf_op jit(solution)/shard_map/while/body/eval_jaxpr/add | solution.py:36
  219.3 2.3 %gather_fusion = f32[256,8]{1,0:T(8,128)S(1)} fusion(f32[8,256,256]{0,2,1:T(8,128)} %copy.39, s32[256]{0:T(256)S(1)} %bitcast.36), kind=kCustom, calls=%fused_computation.clone.clone.1 | custom fusion | bytes 18432 | tf_op jit(solution)/shard_map/while/body/eval_jaxpr/jit(diagonal)/gather | solution.py:38
  221.8 4.8 %fusion.31 = bf16[3,8,256,256]{3,2,1,0:T(8,128)(2,1)} fusion(bf16[3,8,256,256]{3,2,1,0:T(8,128)(2,1)} %get-tuple-element.203, s32[]{:T(128)} %get-tuple-element.202, f32[8,512,512]{2,1,0:T(8,128)} %copy-done, f32[8,256]{1,0:T(8,128)S(1)} %copy.40, pred[256,256]{1,0:T(8,128)(4,1)S(1)} %fusion.30), kind=kLoop, calls=%fused_computation.15.clone.1 | loop fusion | flops 3670016 | bytes 9519616 | tf_op jit(solution)/shard_map/while/body/jit(dynamic_update_index_in_dim)/dynamic_update_slice | solution.py:44
  (51 shorter events, 14.2 us)
Async XLA Ops:
  44.5 13.4 %collective-permute-start = (f32[2,256,8,48]{1,3,2,0:T(8,128)S(1)}, f32[2,256,8,48]{1,3,2,0:T(8,128)}, u32[]{:S(2)}, u32[]{:S(2)}) collective-permute-start(f32[2,256,8,48]{1,3,2,0:T(8,128)S(1)} %copy.32), channel_id=1, source_target_pairs={{1,0},{2,1},{3,2},{4,3},{5,4},{6,5},{7,6},{8,7},{9,8},{10,9},{11,1... | collective-permute-start | bytes 2359304 | tf_op jit(solution)/shard_map/ppermute | solution.py:16
  70.1 1.5 copy-start.1
  94.9 3.2 %copy-start = (f32[8,512,512]{2,1,0:T(8,128)}, f32[8,512,512]{2,1,0:T(8,128)S(1)}, u32[]{:S(2)}) copy-start(f32[8,512,512]{2,1,0:T(8,128)S(1)} %fusion.29) | copy-start | bytes 25165828 | tf_op jit(solution)/shard_map/while
  117.5 4.8 %copy-start.2 = (f32[512,816]{0,1:T(8,128)S(1)}, f32[512,816]{0,1:T(8,128)}, u32[]{:S(2)}) copy-start(f32[512,816]{0,1:T(8,128)} %copy-done.1) | copy-start | bytes 5013508 | tf_op jit(solution)/shard_map/while
  122.3 1.5 copy-start.1
  147.0 3.2 %copy-start = (f32[8,512,512]{2,1,0:T(8,128)}, f32[8,512,512]{2,1,0:T(8,128)S(1)}, u32[]{:S(2)}) copy-start(f32[8,512,512]{2,1,0:T(8,128)S(1)} %fusion.29) | copy-start | bytes 25165828 | tf_op jit(solution)/shard_map/while
  169.6 4.8 %copy-start.2 = (f32[512,816]{0,1:T(8,128)S(1)}, f32[512,816]{0,1:T(8,128)}, u32[]{:S(2)}) copy-start(f32[512,816]{0,1:T(8,128)} %copy-done.1) | copy-start | bytes 5013508 | tf_op jit(solution)/shard_map/while
  174.4 1.5 copy-start.1
  199.1 3.2 %copy-start = (f32[8,512,512]{2,1,0:T(8,128)}, f32[8,512,512]{2,1,0:T(8,128)S(1)}, u32[]{:S(2)}) copy-start(f32[8,512,512]{2,1,0:T(8,128)S(1)} %fusion.29) | copy-start | bytes 25165828 | tf_op jit(solution)/shard_map/while
  221.7 4.8 %copy-start.2 = (f32[512,816]{0,1:T(8,128)S(1)}, f32[512,816]{0,1:T(8,128)}, u32[]{:S(2)}) copy-start(f32[512,816]{0,1:T(8,128)} %copy-done.1) | copy-start | bytes 5013508 | tf_op jit(solution)/shard_map/while
where the time goes:
time: 228 us; the launch traced here: 227 us
  local copies, waits for them, and re-layouts  90.4 us (40%)
  matrix products  69.7 us (31%)
  blocking collectives  28.4 us (12%)
  other arithmetic  22.3 us (10%)
  waiting for transfers between devices  11.4 us (5%)
    dot_general x3, matrix products, one_row(): jnp.einsum('rak,bk->rab', masked, window, precision=lax.Precision.HIGHEST)  69.7 us
    add x3, local copies, waits for them, and re-layouts, one_row(): gram[:, :date_count, :date_count] + gram[:, date_count:, date_count:]  50 us
    all_to_all x1, blocking collectives, on_device(): lax.all_to_all(slc, 'date', split_axis=2, concat_axis=1, tiled=True)  28.4 us
    dynamic_update_slice x3, other arithmetic, coherence_rows(): return lax.map(one_row, jnp.arange(out_rows, dtype=jnp.int32))  14.3 us
    ppermute x1, waiting for transfers between devices, from_behind(): lax.ppermute(value, axis, [(source, source + steps) for source in range(f...  11.4 us
    while x18, local copies, waits for them, and re-layouts  9.62 us
    unnamed x4, local copies, waits for them, and re-layouts  7.41 us
    gather x3, local copies, waits for them, and re-layouts, one_row(): powers = jnp.diagonal(real_part, axis1=1, axis2=2)  6.98 us
  transfers between devices with their start and end apart: 1, of which 1 were waited for; matrix products, arithmetic and copies ran while one was open for 0% of the time, Pallas kernels for 0%

commit v1 on v0

v1 whole, which is shorter than its diff:
```python
import functools

import jax
import jax.numpy as jnp
from jax import lax
from jax.experimental import pallas as pl
from jax.experimental.pallas import tpu as pltpu
from jax.sharding import PartitionSpec as P

BOX_AZ = 11
BOX_RG = 23
STEP_AZ = 3
STEP_RG = 6
MARGIN = 8
LANES = 128
MESH = pl.DeviceIdType.MESH


def round_up(value, multiple):
    return -(-value // multiple) * multiple


def exchange_kernel(axis, count, margin_lanes, x_ref, slab_ref, below_ref, send_sem, recv_sem, fsend_sem, frecv_sem, own_sem):
    me = lax.axis_index(axis)
    before = lax.rem(me + count - 1, count)
    barrier = pltpu.get_barrier_semaphore()

    def greet(step, carry):
        pl.semaphore_signal(barrier, inc=1, device_id={axis: lax.rem(me + step, count)}, device_id_type=MESH)
        return carry

    lax.fori_loop(1, count, greet, 0)
    pl.semaphore_wait(barrier, count - 1)

    def slab_copy(step):
        to = lax.rem(me + step, count)
        return pltpu.make_async_remote_copy(
            src_ref=x_ref.at[to],
            dst_ref=slab_ref.at[:, me],
            send_sem=send_sem.at[step],
            recv_sem=recv_sem.at[step],
            device_id={axis: to},
            device_id_type=MESH,
        )

    def slab_arrival(step):
        source = lax.rem(me + count - step, count)
        return pltpu.make_async_remote_copy(
            src_ref=x_ref.at[source],
            dst_ref=slab_ref.at[:, source],
            send_sem=send_sem.at[step],
            recv_sem=recv_sem.at[step],
            device_id={axis: source},
            device_id_type=MESH,
        )

    def below_copy(step):
        source = lax.rem(me + count - step, count)
        return pltpu.make_async_remote_copy(
            src_ref=slab_ref.at[:, source, :, 0:margin_lanes],
            dst_ref=below_ref.at[:, source],
            send_sem=fsend_sem.at[source],
            recv_sem=frecv_sem.at[source],
            device_id={axis: before},
            device_id_type=MESH,
        )

    def start(step, carry):
        slab_copy(step).start()
        return carry

    lax.fori_loop(1, count, start, 0)
    own = pltpu.make_async_copy(x_ref.at[me], slab_ref.at[:, me], own_sem)
    own.start()
    own.wait()

    @pl.when(me > 0)
    def _():
        below_copy(0).start()

    def arrive(step, carry):
        slab_arrival(step).wait_recv()

        @pl.when(me > 0)
        def _():
            below_copy(step).start()

        return carry

    lax.fori_loop(1, count, arrive, 0)

    def finish(step, carry):
        @pl.when(step > 0)
        def _():
            slab_copy(step).wait_send()

        @pl.when(me > 0)
        def _():
            below_copy(step).wait_send()

        @pl.when(me < count - 1)
        def _():
            below_copy(step).wait_recv()

        return carry

    lax.fori_loop(0, count, finish, 0)


def exchange(messages, axis, margin_lanes):
    count, parts, dates, lanes = messages.shape
    return pl.pallas_call(
        functools.partial(exchange_kernel, axis, count, margin_lanes),
        out_shape=(
            jax.ShapeDtypeStruct((parts, count, dates, lanes), jnp.float32),
            jax.ShapeDtypeStruct((parts, count, dates, margin_lanes), jnp.float32),
        ),
        in_specs=[pl.BlockSpec(memory_space=pl.ANY)],
        out_specs=(pl.BlockSpec(memory_space=pl.ANY), pl.BlockSpec(memory_space=pl.ANY)),
        scratch_shapes=[pltpu.SemaphoreType.DMA((count,))] * 4 + [pltpu.SemaphoreType.DMA],
        compiler_params=pltpu.CompilerParams(collective_id=0, has_side_effects=True),
    )(messages)


def gram_kernel(axis, dates, range_width, slab_lanes, slab_ref, below_ref, pick_ref, out_ref, high, low, partial):
    groups = range_width // STEP_RG
    out_row = pl.program_id(0)

    @pl.when(out_row == 0)
    def _():
        not_last = lax.axis_index(axis) < lax.axis_size(axis) - 1
        below = jnp.where(not_last, below_ref[...], 0.0)
        for at, value in ((0, slab_ref[...]), (slab_lanes, below)):
            big = value.astype(jnp.bfloat16)
            small = (value - big.astype(jnp.float32)).astype(jnp.bfloat16)
            pick = pick_ref[at:at + value.shape[1], :]
            for half, held in ((big, high), (small, low)):
                moved = jnp.dot(half, pick, preferred_element_type=jnp.float32)
                if at == 0:
                    held[...] = moved.astype(jnp.bfloat16)
                else:
                    held[...] = held[...] + moved.astype(jnp.bfloat16)

    lane = lax.broadcasted_iota(jnp.int32, (1, LANES), 1)
    row, column = lane // STEP_RG, lane % STEP_RG
    first = out_row * STEP_AZ
    in_rows = (row >= first) & (row < first + BOX_AZ)
    lower = lax.broadcasted_iota(jnp.int32, (dates, dates), 0)
    upper = lax.broadcasted_iota(jnp.int32, (dates, dates), 1)
    real_side = upper >= lower
    reach = (BOX_RG - 1) // STEP_RG
    short = BOX_RG - reach * STEP_RG

    def packed(group, inside):
        at = pl.ds(group * LANES, LANES)
        rh, rl = high[0:dates, at], low[0:dates, at]
        ih, il = high[dates:, at], low[dates:, at]
        keep = jnp.where(inside, 1.0, 0.0).astype(jnp.bfloat16)
        rhm, rlm, ihm, ilm = rh * keep, rl * keep, ih * keep, il * keep
        right = jnp.concatenate([rh, rl, rh, ih, il, ih], axis=1)
        left_re = jnp.concatenate([rhm, rhm, rlm, ihm, ihm, ilm], axis=1)
        left_im = jnp.concatenate([ihm, ihm, ilm, -rhm, -rhm, -rlm], axis=1)
        dims = (((1,), (1,)), ((), ()))
        real = lax.dot_general(left_re, right, dims, preferred_element_type=jnp.float32)
        imag = lax.dot_general(left_im, right, dims, preferred_element_type=jnp.float32)
        return jnp.where(real_side, real, imag)

    for group in range(groups):
        if group >= reach:
            total = packed(group, in_rows & (column < short))
            write(out_ref, group - reach, [partial[g] for g in range(group - reach, group)] + [total], lower == upper)
            partial[group] = total + packed(group, in_rows & (column >= short))
        else:
            partial[group] = packed(group, in_rows)
    for group in range(max(0, groups - reach), groups):
        write(out_ref, group, [partial[g] for g in range(group, groups)], lower == upper)


def write(out_ref, column, terms, diagonal):
    total = terms[0]
    for term in terms[1:]:
        total = total + term
    power = jnp.where(diagonal, total, 0.0)
    down = 1.0 / jnp.sqrt(jnp.sum(power, axis=1, keepdims=True))
    across = 1.0 / jnp.sqrt(jnp.sum(power, axis=0, keepdims=True))
    out_ref[0, column] = (total * (down * across)).astype(out_ref.dtype)


def coherence_rows(slab, below, axis, out_rows, slab_height, range_width):
    dates = slab.shape[0] // 2
    groups = range_width // STEP_RG
    slab_lanes, margin_lanes = slab.shape[1], below.shape[1]
    source = jnp.arange(slab_lanes + margin_lanes)[:, None]
    target = jnp.arange(groups * LANES)[None]
    group, within = target // LANES, target % LANES
    row, column = within // STEP_RG, group * STEP_RG + within % STEP_RG
    wanted = jnp.where(
        row < slab_height,
        row * range_width + column,
        slab_lanes + (row - slab_height) * range_width + column,
    )
    wanted = jnp.where(row < slab_height + MARGIN, wanted, -1)
    pick = (source == wanted).astype(jnp.bfloat16)
    return pl.pallas_call(
        functools.partial(gram_kernel, axis, dates, range_width, slab_lanes),
        grid=(out_rows,),
        out_shape=jax.ShapeDtypeStruct((out_rows, groups, dates, dates), jnp.bfloat16),
        in_specs=[
            pl.BlockSpec(slab.shape, lambda a: (0, 0)),
            pl.BlockSpec(below.shape, lambda a: (0, 0)),
            pl.BlockSpec(pick.shape, lambda a: (0, 0)),
        ],
        out_specs=pl.BlockSpec((1, groups, dates, dates), lambda a: (a, 0, 0, 0)),
        scratch_shapes=[
            pltpu.VMEM((2 * dates, groups * LANES), jnp.bfloat16),
            pltpu.VMEM((2 * dates, groups * LANES), jnp.bfloat16),
            pltpu.VMEM((groups, dates, dates), jnp.float32),
        ],
        compiler_params=pltpu.CompilerParams(vmem_limit_bytes=48 * 1024 * 1024),
    )(slab, below, pick)


def on_device(slc):
    axis = "date"
    count = lax.axis_size(axis)
    parts, dates, height, width = slc.shape
    slab_height = height // count
    slab = slab_height * width
    messages = slc.reshape(parts, dates, count, slab).transpose(2, 0, 1, 3)
    messages = jnp.pad(messages, ((0, 0),) * 3 + ((0, round_up(slab, LANES) - slab),))
    slabs, below = exchange(messages, axis, MARGIN * width)
    slabs = slabs.reshape(parts * count * dates, -1)
    below = below.reshape(parts * count * dates, -1)
    return coherence_rows(slabs, below, axis, slab_height // STEP_AZ, slab_height, width)


def solution(mesh):
    in_specs = (P(None, "date", "frames", None),)
    out_specs = P(("frames", "date"), None, None, None)
    return jax.shard_map(
        on_device, mesh=mesh, in_specs=in_specs, out_specs=out_specs, check_vma=False
    )
```

time: 228 us -> 59.6 us (0.26)
  the two profiles are of different devices: /device:TPU:9 before, /device:TPU:13 now
where the time goes in v1:
time: 59.6 us; the launch traced here: 59.3 us
  Pallas kernels  49.7 us (83%)
  local copies, waits for them, and re-layouts  8.86 us (15%)
  other arithmetic  0.75 us (1%)
    pallas_call x1, Pallas kernels, exchange(): pl.pallas_call(functools.partial(exchange_kernel, axis, count, margin_lan...  36.9 us
    pallas_call x1, Pallas kernels, coherence_rows(): pl.pallas_call(functools.partial(gram_kernel, axis, dates, range_width, s...  12.7 us
    unnamed x7, local copies, waits for them, and re-layouts  5.05 us
    reshape x2, local copies, waits for them, and re-layouts, on_device(): messages = slc.reshape(parts, dates, count, slab).transpose(2, 0, 1, 3)  2.73 us

profile of v1, /device:TPU:13, one launch (start us, length us, event | category | flops | bytes accessed | tf_op | source)
XLA Modules:
  0.0 59.3 jit_solution(8775089061745502259)
XLA Ops:
  0.0 0.0 copy-start.2
  0.0 0.7 %fusion.pick_ref = bf16[896,1024]{1,0:T(8,128)(2,1)S(1)} fusion(s32[1024]{0:T(1024)S(1)} %select_select_fusion), kind=kLoop, calls=%fused_computation.1 | loop fusion | flops 1835008 | bytes 1839104 | tf_op jit(solution)/shard_map/convert_element_type | solution.py:203
  0.8 0.6 %copy-done.2 = f32[2,16,144,48]{2,3,1,0:T(8,128)S(1)} copy-done((f32[2,16,144,48]{2,3,1,0:T(8,128)S(1)}, f32[2,16,144,48]{2,3,1,0:T(8,128)}, u32[]{:S(2)}) %copy-start.2) | copy-done | bytes 884760
  1.4 2.0 %copy.2 = f32[2,16,144,48]{3,2,1,0:T(8,128)} copy(f32[2,16,144,48]{2,3,1,0:T(8,128)S(1)} %copy-done.2) | data formatting | bytes 1769472 | tf_op args[0]
  3.5 2.1 %reshape.110 = f32[2,16,16,432]{3,2,1,0:T(8,128)S(1)} reshape(f32[2,16,144,48]{3,2,1,0:T(8,128)} %copy.2) | data formatting | bytes 1769472 | tf_op jit(solution)/shard_map/reshape | solution.py:229
  5.6 0.6 %copy.5 = f32[2,16,16,432]{3,1,0,2:T(8,128)S(1)} copy(f32[2,16,16,432]{3,2,1,0:T(8,128)S(1)} %reshape.110) | data formatting | bytes 1769472 | tf_op jit(solution)/shard_map/reshape | solution.py:229
  6.2 1.1 %pad.4.x_ref = f32[16,2,16,512]{3,2,1,0:T(8,128)} pad(f32[16,2,16,432]{3,2,1,0:T(8,128)S(1)} %bitcast.9, f32[]{:T(128)} %constant.45.clone.1), padding=0_0x0_0x0_0x0_80 | pad | bytes 1933316 | tf_op jit(solution)/shard_map/jit(_pad)/pad | solution.py:230
  7.3 36.9 %shard_map.17 = (f32[2,16,16,512]{3,2,1,0:T(8,128)}, f32[2,16,16,384]{3,2,1,0:T(8,128)}) custom-call(f32[16,2,16,512]{3,2,1,0:T(8,128)} %pad.4.x_ref), custom_call_target="tpu_custom_call" | custom-call | tf_op jit(solution)/shard_map/pallas_call | solution.py:112
  44.2 0.0 copy-start
  44.2 1.2 %copy-done = f32[2,16,16,512]{3,2,1,0:T(8,128)S(1)} copy-done((f32[2,16,16,512]{3,2,1,0:T(8,128)S(1)}, f32[2,16,16,512]{3,2,1,0:T(8,128)}, u32[]{:S(2)}) %copy-start) | copy-done | bytes 1048600
  45.4 0.0 copy-start.1
  45.4 1.1 %copy-done.1 = f32[2,16,16,384]{3,2,1,0:T(8,128)S(1)} copy-done((f32[2,16,16,384]{3,2,1,0:T(8,128)S(1)}, f32[2,16,16,384]{3,2,1,0:T(8,128)}, u32[]{:S(2)}) %copy-start.1) | copy-done | bytes 786456
  46.6 12.7 %shard_map.18 = bf16[3,8,256,256]{3,2,1,0:T(8,128)(2,1)} custom-call(f32[512,512]{1,0:T(8,128)S(1)} %bitcast.7, f32[512,384]{1,0:T(8,128)S(1)} %bitcast.8, bf16[896,1024]{1,0:T(8,128)(2,1)S(1)} %fusion.pick_ref), custom_call_target="tpu_custom_call" | custom-call | tf_op jit(solution)/shard_map/pallas_call | solution.py:204
  (1 shorter events, 0.0 us)
Async XLA Ops:
  0.0 1.4 %copy-start.2 = (f32[2,16,144,48]{2,3,1,0:T(8,128)S(1)}, f32[2,16,144,48]{2,3,1,0:T(8,128)}, u32[]{:S(2)}) copy-start(f32[2,16,144,48]{2,3,1,0:T(8,128)} %param.1) | copy-start | bytes 2654212
  44.2 1.2 %copy-start = (f32[2,16,16,512]{3,2,1,0:T(8,128)S(1)}, f32[2,16,16,512]{3,2,1,0:T(8,128)}, u32[]{:S(2)}) copy-start(f32[2,16,16,512]{3,2,1,0:T(8,128)} %get-tuple-element.7) | copy-start | bytes 3145732
  45.4 1.1 %copy-start.1 = (f32[2,16,16,384]{3,2,1,0:T(8,128)S(1)}, f32[2,16,16,384]{3,2,1,0:T(8,128)}, u32[]{:S(2)}) copy-start(f32[2,16,16,384]{3,2,1,0:T(8,128)} %get-tuple-element.8) | copy-start | bytes 2359300

commit v2 on v0

v2 whole, which is shorter than its diff:
```python
import functools

import jax
import jax.numpy as jnp
from jax import lax
from jax.experimental import pallas as pl
from jax.experimental.pallas import tpu as pltpu
from jax.sharding import PartitionSpec as P

BOX_AZ = 11
BOX_RG = 23
STEP_AZ = 3
STEP_RG = 6
MARGIN = 8
LANES = 128
PARTS = 2
MESH = pl.DeviceIdType.MESH
CONTRACT_LANES = (((1,), (1,)), ((), ()))


def round_up(value, multiple):
    return -(-value // multiple) * multiple


def split_in_two(value):
    big = value.astype(jnp.bfloat16)
    return big, (value - big.astype(jnp.float32)).astype(jnp.bfloat16)


def fill_pick(pick, blocks, tail, slab_height, width):
    target = lax.broadcasted_iota(jnp.int32, (1, pick.shape[1]), 1)
    within = target % LANES
    row, column = within // STEP_RG, target // LANES * STEP_RG + within % STEP_RG
    main = blocks * LANES
    wanted = jnp.where(row < MARGIN, row * width + column, main + (row - MARGIN) * width + column)
    below = main + PARTS * tail * LANES
    wanted = jnp.where(row >= slab_height, below + (row - slab_height) * width + column, wanted)
    wanted = jnp.where(row < slab_height + MARGIN, wanted, -1)
    in_tail = (row >= MARGIN) & (row < slab_height)
    tail_width = (slab_height - MARGIN) * width
    other = jnp.where(in_tail, wanted + tail * LANES + tail_width, -1)
    for at in range(0, pick.shape[0], LANES):
        source = at + lax.broadcasted_iota(jnp.int32, (LANES, pick.shape[1]), 0)
        taken = (source == wanted) | (source == other)
        pick[at:at + LANES, :] = jnp.where(taken, 1.0, 0.0).astype(jnp.bfloat16)


def kernel(axis, slab_height, width, x_ref, out_ref, slab, below, pick, high, low, partial, rows_out,
           send_sem, recv_sem, fsend_sem, frecv_sem, own_sem, out_sem):
    count, dates = slab.shape[1], slab.shape[1] * slab.shape[2]
    blocks = below.shape[0] // PARTS
    groups = width // STEP_RG
    out_rows = slab_height // STEP_AZ
    me = lax.axis_index(axis)
    before = lax.rem(me + count - 1, count)
    barrier = pltpu.get_barrier_semaphore()

    def greet(step, carry):
        pl.semaphore_signal(barrier, inc=1, device_id={axis: lax.rem(me + step, count)}, device_id_type=MESH)
        return carry

    lax.fori_loop(1, count, greet, 0)
    pl.semaphore_wait(barrier, count - 1)

    def slab_copy(step, to, source):
        return pltpu.make_async_remote_copy(
            src_ref=x_ref.at[to],
            dst_ref=slab.at[:, source],
            send_sem=send_sem.at[step],
            recv_sem=recv_sem.at[step],
            device_id={axis: to},
            device_id_type=MESH,
        )

    def below_copy(block):
        return pltpu.make_async_remote_copy(
            src_ref=slab.at[pl.ds(PARTS * block, PARTS)],
            dst_ref=below.at[pl.ds(PARTS * block, PARTS)],
            send_sem=fsend_sem.at[block],
            recv_sem=frecv_sem.at[block],
            device_id={axis: before},
            device_id_type=MESH,
        )

    def start(step, carry):
        slab_copy(step, lax.rem(me + step, count), me).start()
        return carry

    lax.fori_loop(1, count, start, 0)
    own = pltpu.make_async_copy(x_ref.at[me], slab.at[:, me], own_sem)
    own.start()
    fill_pick(pick, blocks, 1, slab_height, width)
    own.wait()

    def arrive(step, carry):
        source = lax.rem(me + count - step, count)
        slab_copy(step, source, source).wait_recv()
        return carry

    lax.fori_loop(1, count, arrive, 0)

    @pl.when(me > 0)
    def _():
        for block in range(blocks):
            below_copy(block).start()

    for part in range(PARTS):
        tiles = [PARTS * block + part for block in range(blocks)] + [PARTS * blocks]
        value = jnp.concatenate([slab[t].reshape(dates, LANES) for t in tiles], axis=1)
        main = blocks * LANES
        mine = jnp.concatenate([pick[0:main, :], pick[main + part * LANES:main + (part + 1) * LANES, :]], axis=0)
        for half, held in zip(split_in_two(value), (high, low)):
            moved = jnp.dot(half, mine, preferred_element_type=jnp.float32)
            held[part * dates:(part + 1) * dates, :] = moved.astype(jnp.bfloat16)

    lane = lax.broadcasted_iota(jnp.int32, (1, LANES), 1)
    row, column = lane // STEP_RG, lane % STEP_RG
    lower = lax.broadcasted_iota(jnp.int32, (dates, dates), 0)
    upper = lax.broadcasted_iota(jnp.int32, (dates, dates), 1)
    reach = (BOX_RG - 1) // STEP_RG
    short = BOX_RG - reach * STEP_RG

    def packed(group, inside):
        at = slice(group * LANES, (group + 1) * LANES)
        rh, rl = high[0:dates, at], low[0:dates, at]
        ih, il = high[dates:, at], low[dates:, at]
        keep = jnp.where(inside, 1.0, 0.0).astype(jnp.bfloat16)
        rhm, rlm, ihm, ilm = rh * keep, rl * keep, ih * keep, il * keep
        right = jnp.concatenate([rh, rl, rh, ih, il, ih], axis=1)
        left_re = jnp.concatenate([rhm, rhm, rlm, ihm, ihm, ilm], axis=1)
        left_im = jnp.concatenate([ihm, ihm, ilm, -rhm, -rhm, -rlm], axis=1)
        real = lax.dot_general(left_re, right, CONTRACT_LANES, preferred_element_type=jnp.float32)
        imag = lax.dot_general(left_im, right, CONTRACT_LANES, preferred_element_type=jnp.float32)
        return jnp.where(upper >= lower, real, imag)

    def out_copy(out_row, at):
        return pltpu.make_async_copy(rows_out.at[out_row, at], out_ref.at[out_row, at], out_sem.at[out_row, at])

    def write(out_row, at, terms):
        total = terms[0]
        for term in terms[1:]:
            total = total + term
        power = jnp.where(upper == lower, total, 0.0)
        down = 1.0 / jnp.sqrt(jnp.sum(power, axis=1, keepdims=True))
        across = 1.0 / jnp.sqrt(jnp.sum(power, axis=0, keepdims=True))
        rows_out[out_row, at] = (total * (down * across)).astype(rows_out.dtype)
        out_copy(out_row, at).start()

    def one_row(out_row, carry):
        @pl.when(me < count - 1)
        def _():
            below_copy(out_row).wait_recv()
            at = (blocks + PARTS) * LANES + out_row * LANES
            mine = pick[pl.ds(pl.multiple_of(at, LANES), LANES), :]
            for part in range(PARTS):
                value = below[PARTS * out_row + part].reshape(dates, LANES)
                for half, held in zip(split_in_two(value), (high, low)):
                    moved = jnp.dot(half, mine, preferred_element_type=jnp.float32)
                    here = slice(part * dates, (part + 1) * dates)
                    held[here, :] = held[here, :] + moved.astype(jnp.bfloat16)

        first = out_row * STEP_AZ
        in_rows = (row >= first) & (row < first + BOX_AZ)
        for group in range(groups):
            if group >= reach:
                total = packed(group, in_rows & (column < short))
                write(out_row, group - reach, [partial[g] for g in range(group - reach, group)] + [total])
                partial[group] = total + packed(group, in_rows & (column >= short))
            else:
                partial[group] = packed(group, in_rows)
        for group in range(max(0, groups - reach), groups):
            write(out_row, group, [partial[g] for g in range(group, groups)])
        return carry

    lax.fori_loop(0, out_rows, one_row, 0)

    def sent(step, carry):
        slab_copy(step, lax.rem(me + step, count), me).wait_send()
        return carry

    lax.fori_loop(1, count, sent, 0)

    @pl.when(me > 0)
    def _():
        for block in range(blocks):
            below_copy(block).wait_send()

    def written(out_row, carry):
        for at in range(groups):
            out_copy(out_row, at).wait()
        return carry

    lax.fori_loop(0, out_rows, written, 0)


def on_device(slc):
    axis = "date"
    count = lax.axis_size(axis)
    parts, own_dates, height, width = slc.shape
    slab_height = height // count
    out_rows = slab_height // STEP_AZ
    main, tail = MARGIN * width, (slab_height - MARGIN) * width
    blocks = main // LANES
    groups = width // STEP_RG
    dates = count * own_dates
    assert main % LANES == 0 and parts * tail <= LANES and blocks == out_rows
    slabs = slc.reshape(parts, own_dates, count, slab_height * width)
    first = slabs[..., :main].reshape(parts, own_dates, count, blocks, LANES)
    first = first.transpose(2, 3, 0, 1, 4).reshape(count, blocks * parts, own_dates, LANES)
    last = slabs[..., main:].transpose(2, 1, 0, 3).reshape(count, 1, own_dates, parts * tail)
    last = jnp.pad(last, ((0, 0),) * 3 + ((0, LANES - parts * tail),))
    messages = jnp.concatenate([first, last], axis=1)
    wide = groups * LANES
    return pl.pallas_call(
        functools.partial(kernel, axis, slab_height, width),
        out_shape=jax.ShapeDtypeStruct((out_rows, groups, dates, dates), jnp.bfloat16),
        in_specs=[pl.BlockSpec(memory_space=pltpu.VMEM)],
        out_specs=pl.BlockSpec(memory_space=pl.ANY),
        scratch_shapes=[
            pltpu.VMEM((parts * blocks + 1, count, own_dates, LANES), jnp.float32),
            pltpu.VMEM((parts * blocks, count, own_dates, LANES), jnp.float32),
            pltpu.VMEM(((2 * blocks + parts) * LANES, wide), jnp.bfloat16),
            pltpu.VMEM((parts * dates, wide), jnp.bfloat16),
            pltpu.VMEM((parts * dates, wide), jnp.bfloat16),
            pltpu.VMEM((groups, dates, dates), jnp.float32),
            pltpu.VMEM((out_rows, groups, dates, dates), jnp.bfloat16),
            pltpu.SemaphoreType.DMA((count,)),
            pltpu.SemaphoreType.DMA((count,)),
            pltpu.SemaphoreType.DMA((blocks,)),
            pltpu.SemaphoreType.DMA((blocks,)),
            pltpu.SemaphoreType.DMA,
            pltpu.SemaphoreType.DMA((out_rows, groups)),
        ],
        compiler_params=pltpu.CompilerParams(
            collective_id=0, has_side_effects=True, vmem_limit_bytes=48 * 1024 * 1024
        ),
    )(messages)


def solution(mesh):
    in_specs = (P(None, "date", "frames", None),)
    out_specs = P(("frames", "date"), None, None, None)
    return jax.shard_map(
        on_device, mesh=mesh, in_specs=in_specs, out_specs=out_specs, check_vma=False
    )
```

time: 228 us -> 56.5 us (0.25)
  local copies, waits for them, and re-layouts: 90.4 us -> 5.66 us
  matrix products: 69.7 us -> 0 us
  Pallas kernels: 0 us -> 50.6 us
  blocking collectives: 28.4 us -> 0 us
  other arithmetic: 22.3 us -> 0.07 us
  waiting for transfers between devices: 11.4 us -> 0 us
    dot_general x3 -> x0, matrix products: 69.7 us -> none  [one_row(): jnp.einsum('rak,bk->rab', masked, window, precision=lax.Precision.HIGHEST)]
    pallas_call x0 -> x1, Pallas kernels: none -> 50.6 us  [on_device(): pl.pallas_call(functools.partial(kernel, axis, slab_height, width), out_s...]
    add x3 -> x0, local copies, waits for them, and re-layouts: 50 us -> none  [one_row(): gram[:, :date_count, :date_count] + gram[:, date_count:, date_count:]]
    all_to_all x1 -> x0, blocking collectives: 28.4 us -> none  [on_device(): lax.all_to_all(slc, 'date', split_axis=2, concat_axis=1, tiled=True)]
    dynamic_update_slice x3 -> x0, other arithmetic: 14.3 us -> none  [coherence_rows(): return lax.map(one_row, jnp.arange(out_rows, dtype=jnp.int32))]
    ppermute x1 -> x0, waiting for transfers between devices: 11.4 us -> none  [from_behind(): lax.ppermute(value, axis, [(source, source + steps) for source in range(f...]
    while x18 -> x0, local copies, waits for them, and re-layouts: 9.62 us -> none
    gather x3 -> x0, local copies, waits for them, and re-layouts: 6.98 us -> none  [one_row(): powers = jnp.diagonal(real_part, axis1=1, axis2=2)]
  transfers between devices with their start and end apart: 1 -> 0, of which waited for: 1 -> 0; matrix products, arithmetic and copies ran while one was open for 0% -> 0% of each run, Pallas kernels for 0% -> 0%
where the time goes in v2:
time: 56.5 us; the launch traced here: 56.4 us
  Pallas kernels  50.6 us (90%)
  local copies, waits for them, and re-layouts  5.66 us (10%)
    pallas_call x1, Pallas kernels, on_device(): pl.pallas_call(functools.partial(kernel, axis, slab_height, width), out_s...  50.6 us
    unnamed x2, local copies, waits for them, and re-layouts  3.72 us

profile of v2, /device:TPU:9, one launch (start us, length us, event | category | flops | bytes accessed | tf_op | source)
XLA Modules:
  0.0 56.4 jit_solution(711007712368659733)
XLA Ops:
  0.0 2.1 %copy.3 = f32[2,16,144,48]{3,2,1,0:T(8,128)S(1)} copy(f32[2,16,144,48]{2,3,1,0:T(8,128)} %param.1) | data formatting | bytes 1769472 | tf_op args[0]
  2.1 0.7 %reshape.12 = f32[2,16,16,432]{3,2,1,0:T(8,128)S(1)} reshape(f32[2,16,144,48]{3,2,1,0:T(8,128)S(1)} %copy.3) | data formatting | bytes 1769472 | tf_op jit(solution)/shard_map/reshape | solution.py:207
  2.8 0.1 slice.8
  2.9 0.2 copy.5
  3.1 0.2 reshape.15
  3.3 0.3 reshape.13
  3.6 0.5 copy.4
  4.0 0.1 select_maximum_fusion.x_ref
  4.1 50.6 %shard_map.17 = bf16[3,8,256,256]{3,2,1,0:T(8,128)(2,1)S(1)} custom-call(f32[16,7,16,128]{3,2,1,0:T(8,128)S(1)} %select_maximum_fusion.x_ref), custom_call_target="tpu_custom_call" | custom-call | tf_op jit(solution)/shard_map/pallas_call | solution.py:214
  54.7 1.7 %copy.7 = bf16[3,8,256,256]{3,2,1,0:T(8,128)(2,1)} copy(bf16[3,8,256,256]{3,2,1,0:T(8,128)(2,1)S(1)} %shard_map.17) | data formatting | bytes 6291456
  (1 shorter events, 0.0 us)

commit v3 on v2

--- a/solution.py
+++ b/solution.py
@@ -45,8 +45,8 @@
         pick[at:at + LANES, :] = jnp.where(taken, 1.0, 0.0).astype(jnp.bfloat16)
 
 
-def kernel(axis, slab_height, width, x_ref, out_ref, slab, below, pick, high, low, partial, rows_out,
-           send_sem, recv_sem, fsend_sem, frecv_sem, own_sem, out_sem):
+def kernel(axis, slab_height, width, x_ref, out_ref, slab, below, pick, high, low, partial,
+           send_sem, recv_sem, fsend_sem, frecv_sem, own_sem):
     count, dates = slab.shape[1], slab.shape[1] * slab.shape[2]
     blocks = below.shape[0] // PARTS
     groups = width // STEP_RG
@@ -115,8 +115,10 @@
 
     lane = lax.broadcasted_iota(jnp.int32, (1, LANES), 1)
     row, column = lane // STEP_RG, lane % STEP_RG
-    lower = lax.broadcasted_iota(jnp.int32, (dates, dates), 0)
-    upper = lax.broadcasted_iota(jnp.int32, (dates, dates), 1)
+    half_dates = dates // 2
+    lower = lax.broadcasted_iota(jnp.int32, (half_dates, half_dates), 0)
+    upper = lax.broadcasted_iota(jnp.int32, (half_dates, half_dates), 1)
+    real_side, diagonal = upper >= lower, upper == lower
     reach = (BOX_RG - 1) // STEP_RG
     short = BOX_RG - reach * STEP_RG
 
@@ -129,22 +131,43 @@
         right = jnp.concatenate([rh, rl, rh, ih, il, ih], axis=1)
         left_re = jnp.concatenate([rhm, rhm, rlm, ihm, ihm, ilm], axis=1)
         left_im = jnp.concatenate([ihm, ihm, ilm, -rhm, -rhm, -rlm], axis=1)
-        real = lax.dot_general(left_re, right, CONTRACT_LANES, preferred_element_type=jnp.float32)
-        imag = lax.dot_general(left_im, right, CONTRACT_LANES, preferred_element_type=jnp.float32)
-        return jnp.where(upper >= lower, real, imag)
-
-    def out_copy(out_row, at):
-        return pltpu.make_async_copy(rows_out.at[out_row, at], out_ref.at[out_row, at], out_sem.at[out_row, at])
+
+        def dot(left, right):
+            return lax.dot_general(left, right, CONTRACT_LANES, preferred_element_type=jnp.float32)
+
+        top = dot(left_re[:half_dates], right)
+        bottom = dot(left_im[half_dates:], right)
+        top_imag = dot(left_im[:half_dates], right[:half_dates])
+        bottom_real = dot(left_re[half_dates:], right[half_dates:])
+        return (
+            jnp.where(real_side, top[:, :half_dates], top_imag),
+            top[:, half_dates:],
+            bottom[:, :half_dates],
+            jnp.where(real_side, bottom_real, bottom[:, half_dates:]),
+        )
+
+    def held_partial(group):
+        return tuple(partial[group, block] for block in range(4))
+
+    def hold_partial(group, blocks_of):
+        for block in range(4):
+            partial[group, block] = blocks_of[block]
+
+    def add(one, two):
+        return tuple(a + b for a, b in zip(one, two))
 
     def write(out_row, at, terms):
-        total = terms[0]
-        for term in terms[1:]:
-            total = total + term
-        power = jnp.where(upper == lower, total, 0.0)
-        down = 1.0 / jnp.sqrt(jnp.sum(power, axis=1, keepdims=True))
-        across = 1.0 / jnp.sqrt(jnp.sum(power, axis=0, keepdims=True))
-        rows_out[out_row, at] = (total * (down * across)).astype(rows_out.dtype)
-        out_copy(out_row, at).start()
+        total = functools.reduce(add, terms)
+        down, across = [], []
+        for block in (total[0], total[3]):
+            power = jnp.where(diagonal, block, 0.0)
+            down.append(lax.rsqrt(jnp.sum(power, axis=1, keepdims=True)))
+            across.append(lax.rsqrt(jnp.sum(power, axis=0, keepdims=True)))
+        for block in range(4):
+            m, n = block // 2, block % 2
+            scaled = total[block] * (down[m] * across[n])
+            out_ref[out_row, at, m * half_dates:(m + 1) * half_dates, n * half_dates:(n + 1) * half_dates] = (
+                scaled.astype(out_ref.dtype))
 
     def one_row(out_row, carry):
         @pl.when(me < count - 1)
@@ -164,12 +187,12 @@
         for group in range(groups):
             if group >= reach:
                 total = packed(group, in_rows & (column < short))
-                write(out_row, group - reach, [partial[g] for g in range(group - reach, group)] + [total])
-                partial[group] = total + packed(group, in_rows & (column >= short))
+                write(out_row, group - reach, [held_partial(g) for g in range(group - reach, group)] + [total])
+                hold_partial(group, add(total, packed(group, in_rows & (column >= short))))
             else:
-                partial[group] = packed(group, in_rows)
+                hold_partial(group, packed(group, in_rows))
         for group in range(max(0, groups - reach), groups):
-            write(out_row, group, [partial[g] for g in range(group, groups)])
+            write(out_row, group, [held_partial(g) for g in range(group, groups)])
         return carry
 
     lax.fori_loop(0, out_rows, one_row, 0)
@@ -184,13 +207,6 @@
     def _():
         for block in range(blocks):
             below_copy(block).wait_send()
-
-    def written(out_row, carry):
-        for at in range(groups):
-            out_copy(out_row, at).wait()
-        return carry
-
-    lax.fori_loop(0, out_rows, written, 0)
 
 
 def on_device(slc):
@@ -215,21 +231,19 @@
         functools.partial(kernel, axis, slab_height, width),
         out_shape=jax.ShapeDtypeStruct((out_rows, groups, dates, dates), jnp.bfloat16),
         in_specs=[pl.BlockSpec(memory_space=pltpu.VMEM)],
-        out_specs=pl.BlockSpec(memory_space=pl.ANY),
+        out_specs=pl.BlockSpec(memory_space=pltpu.VMEM),
         scratch_shapes=[
             pltpu.VMEM((parts * blocks + 1, count, own_dates, LANES), jnp.float32),
             pltpu.VMEM((parts * blocks, count, own_dates, LANES), jnp.float32),
             pltpu.VMEM(((2 * blocks + parts) * LANES, wide), jnp.bfloat16),
             pltpu.VMEM((parts * dates, wide), jnp.bfloat16),
             pltpu.VMEM((parts * dates, wide), jnp.bfloat16),
-            pltpu.VMEM((groups, dates, dates), jnp.float32),
-            pltpu.VMEM((out_rows, groups, dates, dates), jnp.bfloat16),
+            pltpu.VMEM((groups, 4, dates // 2, dates // 2), jnp.float32),
             pltpu.SemaphoreType.DMA((count,)),
             pltpu.SemaphoreType.DMA((count,)),
             pltpu.SemaphoreType.DMA((blocks,)),
             pltpu.SemaphoreType.DMA((blocks,)),
             pltpu.SemaphoreType.DMA,
-            pltpu.SemaphoreType.DMA((out_rows, groups)),
         ],
         compiler_params=pltpu.CompilerParams(
             collective_id=0, has_side_effects=True, vmem_limit_bytes=48 * 1024 * 1024

time: 56.5 us -> 53.5 us (0.947)
  Pallas kernels: 50.6 us -> 47.6 us
    pallas_call x1, Pallas kernels: 50.6 us -> 47.6 us  [on_device(): pl.pallas_call(functools.partial(kernel, axis, slab_height, width), out_s...]
where the time goes in v3:
time: 53.5 us; the launch traced here: 53.4 us
  Pallas kernels  47.6 us (89%)
  local copies, waits for them, and re-layouts  5.66 us (11%)
    pallas_call x1, Pallas kernels, on_device(): pl.pallas_call(functools.partial(kernel, axis, slab_height, width), out_s...  47.6 us
    unnamed x2, local copies, waits for them, and re-layouts  3.72 us

profile of v3, /device:TPU:9, one launch (start us, length us, event | category | flops | bytes accessed | tf_op | source)
XLA Modules:
  0.0 53.4 jit_solution(1702916008089063710)
XLA Ops:
  0.0 2.1 %copy.3 = f32[2,16,144,48]{3,2,1,0:T(8,128)S(1)} copy(f32[2,16,144,48]{2,3,1,0:T(8,128)} %param.1) | data formatting | bytes 1769472 | tf_op args[0]
  2.1 0.7 %reshape.12 = f32[2,16,16,432]{3,2,1,0:T(8,128)S(1)} reshape(f32[2,16,144,48]{3,2,1,0:T(8,128)S(1)} %copy.3) | data formatting | bytes 1769472 | tf_op jit(solution)/shard_map/reshape | solution.py:223
  2.8 0.1 slice.8
  2.9 0.2 copy.5
  3.1 0.2 reshape.15
  3.3 0.3 reshape.13
  3.6 0.5 copy.4
  4.0 0.1 select_maximum_fusion.x_ref
  4.1 47.6 %shard_map.17 = bf16[3,8,256,256]{3,2,1,0:T(8,128)(2,1)S(1)} custom-call(f32[16,7,16,128]{3,2,1,0:T(8,128)S(1)} %select_maximum_fusion.x_ref), custom_call_target="tpu_custom_call" | custom-call | tf_op jit(solution)/shard_map/pallas_call | solution.py:230
  51.7 1.7 %copy.7 = bf16[3,8,256,256]{3,2,1,0:T(8,128)(2,1)} copy(bf16[3,8,256,256]{3,2,1,0:T(8,128)(2,1)S(1)} %shard_map.17) | data formatting | bytes 6291456
  (1 shorter events, 0.0 us)

commit v4 on v3

--- a/solution.py
+++ b/solution.py
@@ -122,29 +122,40 @@
     reach = (BOX_RG - 1) // STEP_RG
     short = BOX_RG - reach * STEP_RG
 
-    def packed(group, inside):
+    def packed(group, insides):
         at = slice(group * LANES, (group + 1) * LANES)
         rh, rl = high[0:dates, at], low[0:dates, at]
         ih, il = high[dates:, at], low[dates:, at]
-        keep = jnp.where(inside, 1.0, 0.0).astype(jnp.bfloat16)
-        rhm, rlm, ihm, ilm = rh * keep, rl * keep, ih * keep, il * keep
         right = jnp.concatenate([rh, rl, rh, ih, il, ih], axis=1)
-        left_re = jnp.concatenate([rhm, rhm, rlm, ihm, ihm, ilm], axis=1)
-        left_im = jnp.concatenate([ihm, ihm, ilm, -rhm, -rhm, -rlm], axis=1)
-
-        def dot(left, right):
+        full, top_imag, bottom_real = [], [], []
+        for inside in insides:
+            keep = jnp.where(inside, 1.0, 0.0).astype(jnp.bfloat16)
+            rhm, rlm, ihm, ilm = rh * keep, rl * keep, ih * keep, il * keep
+            left_re = jnp.concatenate([rhm, rhm, rlm, ihm, ihm, ilm], axis=1)
+            left_im = jnp.concatenate([ihm, ihm, ilm, -rhm, -rhm, -rlm], axis=1)
+            full += [left_re[:half_dates], left_im[half_dates:]]
+            top_imag.append(left_im[:half_dates])
+            bottom_real.append(left_re[half_dates:])
+
+        def dot(lefts, right):
+            left = jnp.concatenate(lefts, axis=0)
             return lax.dot_general(left, right, CONTRACT_LANES, preferred_element_type=jnp.float32)
 
-        top = dot(left_re[:half_dates], right)
-        bottom = dot(left_im[half_dates:], right)
-        top_imag = dot(left_im[:half_dates], right[:half_dates])
-        bottom_real = dot(left_re[half_dates:], right[half_dates:])
-        return (
-            jnp.where(real_side, top[:, :half_dates], top_imag),
-            top[:, half_dates:],
-            bottom[:, :half_dates],
-            jnp.where(real_side, bottom_real, bottom[:, half_dates:]),
-        )
+        full = dot(full, right)
+        top_imag = dot(top_imag, right[:half_dates])
+        bottom_real = dot(bottom_real, right[half_dates:])
+        blocks_of = []
+        for index in range(len(insides)):
+            here = slice(index * half_dates, (index + 1) * half_dates)
+            top = full[2 * index * half_dates:(2 * index + 1) * half_dates]
+            bottom = full[(2 * index + 1) * half_dates:(2 * index + 2) * half_dates]
+            blocks_of.append((
+                jnp.where(real_side, top[:, :half_dates], top_imag[here]),
+                top[:, half_dates:],
+                bottom[:, :half_dates],
+                jnp.where(real_side, bottom_real[here], bottom[:, half_dates:]),
+            ))
+        return blocks_of
 
     def held_partial(group):
         return tuple(partial[group, block] for block in range(4))
@@ -186,11 +197,11 @@
         in_rows = (row >= first) & (row < first + BOX_AZ)
         for group in range(groups):
             if group >= reach:
-                total = packed(group, in_rows & (column < short))
+                total, rest = packed(group, [in_rows & (column < short), in_rows & (column >= short)])
                 write(out_row, group - reach, [held_partial(g) for g in range(group - reach, group)] + [total])
-                hold_partial(group, add(total, packed(group, in_rows & (column >= short))))
+                hold_partial(group, add(total, rest))
             else:
-                hold_partial(group, packed(group, in_rows))
+                hold_partial(group, packed(group, [in_rows])[0])
         for group in range(max(0, groups - reach), groups):
             write(out_row, group, [held_partial(g) for g in range(group, groups)])
         return carry

time: 53.5 us -> 47.3 us (0.88)
  Pallas kernels: 47.6 us -> 41.4 us
    pallas_call x1, Pallas kernels: 47.6 us -> 41.4 us  [on_device(): pl.pallas_call(functools.partial(kernel, axis, slab_height, width), out_s...]
where the time goes in v4:
time: 47.3 us; the launch traced here: 47.2 us
  Pallas kernels  41.4 us (88%)
  local copies, waits for them, and re-layouts  5.66 us (12%)
    pallas_call x1, Pallas kernels, on_device(): pl.pallas_call(functools.partial(kernel, axis, slab_height, width), out_s...  41.4 us
    unnamed x2, local copies, waits for them, and re-layouts  3.72 us

profile of v4, /device:TPU:9, one launch (start us, length us, event | category | flops | bytes accessed | tf_op | source)
XLA Modules:
  0.0 47.2 jit_solution(7600266517808517818)
XLA Ops:
  0.0 2.1 %copy.3 = f32[2,16,144,48]{3,2,1,0:T(8,128)S(1)} copy(f32[2,16,144,48]{2,3,1,0:T(8,128)} %param.1) | data formatting | bytes 1769472 | tf_op args[0]
  2.1 0.7 %reshape.12 = f32[2,16,16,432]{3,2,1,0:T(8,128)S(1)} reshape(f32[2,16,144,48]{3,2,1,0:T(8,128)S(1)} %copy.3) | data formatting | bytes 1769472 | tf_op jit(solution)/shard_map/reshape | solution.py:234
  2.8 0.1 slice.8
  2.9 0.2 copy.5
  3.1 0.2 reshape.15
  3.3 0.3 reshape.13
  3.6 0.5 copy.4
  4.0 0.1 select_maximum_fusion.x_ref
  4.1 41.4 %shard_map.17 = bf16[3,8,256,256]{3,2,1,0:T(8,128)(2,1)S(1)} custom-call(f32[16,7,16,128]{3,2,1,0:T(8,128)S(1)} %select_maximum_fusion.x_ref), custom_call_target="tpu_custom_call" | custom-call | tf_op jit(solution)/shard_map/pallas_call | solution.py:241
  45.5 1.7 %copy.7 = bf16[3,8,256,256]{3,2,1,0:T(8,128)(2,1)} copy(bf16[3,8,256,256]{3,2,1,0:T(8,128)(2,1)S(1)} %shard_map.17) | data formatting | bytes 6291456
  (1 shorter events, 0.0 us)
